TPU v7x, 32 devices: a whole 2x2x4 slice. The times are simulated.
32 devices in a mesh: hot: 8 (over y, x, core), load: 4 (over z).
Axes of the slice: x: 2, y: 2, z: 4, core: 2. Of those that a mesh axis runs over, the one named last changes fastest.
Arguments:
- response: bfloat16 [2048, 2048, 128], P('hot', 'load'), may hold values from -1 to 1, as said below
- forces: bfloat16 [2048, 1408], P('load'), may hold values from -6 to 6
- measured: float32 [2048, 384], P('hot'), may hold values from -6 to 6
Outputs:
- updated_forces: float32 [2048, 1408], P('load')
- updated_residual: float32 [2048, 384], P('hot')
Inputs may be any that keep to these rules, and one draw needn't show every extreme that they name: impulse-response coefficients.
All inputs are finite; a program needn't handle non-finite values.
Results may differ from a plain program's by a relative error of at most 0.0041.
Values sent between devices are 32-bit elements; how exact they have to be, the bound alone decides.
A program may use at most 448 MiB of HBM per device.

v0:
```python
import jax
import jax.numpy as jnp
from jax import lax
from jax.sharding import PartitionSpec as P

TAPS = 128
SEG = 48
CASES = 8
HIST = 128
STEPS = 176


def strain_product(response, signal):
    seg_cols = SEG * CASES
    running = jnp.zeros((response.shape[0], seg_cols), jnp.float32)
    tap_span = min(16, TAPS)
    for first_tap in range(0, TAPS, tap_span):
        window = jnp.stack(
            [
                signal[:, (HIST - tap_index) * CASES : (HIST - tap_index) * CASES + seg_cols]
                for tap_index in range(first_tap, first_tap + tap_span)
            ],
            axis=1,
        )
        running = running + jnp.einsum(
            "hlk,lkm->hm",
            response[:, :, first_tap : first_tap + tap_span],
            window,
            preferred_element_type=jnp.float32,
        )
    return running


def load_product(response, strains):
    col_count = STEPS * CASES
    padded = jnp.pad(strains, ((0, 0), (HIST * CASES, TAPS * CASES)))
    running = jnp.zeros((response.shape[1], col_count), jnp.float32)
    tap_span = min(16, TAPS)
    for first_tap in range(0, TAPS, tap_span):
        window = jnp.stack(
            [
                padded[:, tap_index * CASES : tap_index * CASES + col_count]
                for tap_index in range(first_tap, first_tap + tap_span)
            ],
            axis=1,
        )
        running = running + jnp.einsum(
            "hlk,hkm->lm",
            response[:, :, first_tap : first_tap + tap_span],
            window,
            preferred_element_type=jnp.float32,
        )
    return running


def body(response, forces, measured):
    strains = lax.psum(strain_product(response, forces), "load")
    residual = measured - strains
    residual_b = residual.astype(jnp.bfloat16)
    gradient = lax.psum(load_product(response, residual_b), "hot")
    grad_local = jnp.sum(gradient * gradient)
    grad_total = lax.psum(grad_local, "load")
    gradient_b = gradient.astype(jnp.bfloat16)
    image_sum = lax.psum(strain_product(response, gradient_b), "load")
    image_local = jnp.sum(image_sum * image_sum)
    image_total = lax.psum(image_local, "hot")
    step_size = grad_total / image_total
    return (forces.astype(jnp.float32) + step_size * gradient, residual - step_size * image_sum)


def solution(mesh):
    placed = (P("hot", "load", None), P("load", None), P("hot", None))
    return jax.shard_map(
        body,
        mesh=mesh,
        in_specs=placed,
        out_specs=(P("load", None), P("hot", None)),
        check_vma=False,
    )
```

profile of v0, /device:TPU:0, one launch (start us, length us, event | category | flops | bytes accessed | tf_op | source)
XLA Modules:
  0.0 851.9 jit_solution(18117567018206587305)
XLA Ops:
  7.2 1.7 copy.5
  8.9 1.6 constant_dynamic-update-slice_fusion.111
  10.5 180.4 %fusion.153 = (bf16[256,512,16]{2,1,0:T(8,128)(2,1)}, bf16[256,512,16]{2,1,0:T(8,128)(2,1)}, bf16[256,512,16]{2,1,0:T(8,128)(2,1)}, bf16[256,512,16]{2,1,0:T(8,1...) fusion(bf16[256,512,128]{2,1,0:T(8,128)(2,1)} %param.3), kind=kLoop, calls=%fused_computation.949 | loop fusion | bytes 67108864 | tf_op jit(solution)/shard_map/slice | solution.py:27
  190.9 26.9 %copy.146 = bf16[256,512,16]{1,0,2:T(8,128)(2,1)} copy(bf16[256,512,16]{2,1,0:T(8,128)(2,1)} %get-tuple-element.12) | data formatting | bytes 8388608
  217.8 26.9 %copy.145 = bf16[256,512,16]{1,0,2:T(8,128)(2,1)} copy(bf16[256,512,16]{2,1,0:T(8,128)(2,1)} %get-tuple-element.13) | data formatting | bytes 8388608
  244.7 26.9 %copy.147 = bf16[256,512,16]{1,0,2:T(8,128)(2,1)} copy(bf16[256,512,16]{2,1,0:T(8,128)(2,1)} %get-tuple-element.11) | data formatting | bytes 8388608
  271.7 26.9 %copy.148 = bf16[256,512,16]{1,0,2:T(8,128)(2,1)} copy(bf16[256,512,16]{2,1,0:T(8,128)(2,1)} %get-tuple-element.10) | data formatting | bytes 8388608
  298.6 26.9 %copy.149 = bf16[256,512,16]{1,0,2:T(8,128)(2,1)} copy(bf16[256,512,16]{2,1,0:T(8,128)(2,1)} %get-tuple-element.9) | data formatting | bytes 8388608
  325.5 26.9 %copy.150 = bf16[256,512,16]{1,0,2:T(8,128)(2,1)} copy(bf16[256,512,16]{2,1,0:T(8,128)(2,1)} %get-tuple-element.8) | data formatting | bytes 8388608
  352.4 27.0 %copy.151 = bf16[256,512,16]{1,0,2:T(8,128)(2,1)} copy(bf16[256,512,16]{2,1,0:T(8,128)(2,1)} %get-tuple-element.7) | data formatting | bytes 8388608
  379.4 1.6 constant_dynamic-update-slice_fusion.127
  381.0 1.6 constant_dynamic-update-slice_fusion.126
  382.5 1.6 constant_dynamic-update-slice_fusion.125
  384.1 1.6 constant_dynamic-update-slice_fusion.124
  385.7 1.6 constant_dynamic-update-slice_fusion.123
  387.3 1.6 constant_dynamic-update-slice_fusion.122
  388.9 1.6 constant_dynamic-update-slice_fusion.121
  390.5 1.6 constant_dynamic-update-slice_fusion.120
  393.6 1.6 constant_dynamic-update-slice_fusion.118
  395.2 1.6 constant_dynamic-update-slice_fusion.117
  396.8 1.6 constant_dynamic-update-slice_fusion.116
  398.4 1.6 constant_dynamic-update-slice_fusion.115
  399.9 1.6 constant_dynamic-update-slice_fusion.114
  403.1 2.6 copy-done.29
  405.7 27.5 %copy.152 = bf16[256,512,16]{1,0,2:T(8,128)(2,1)} copy(bf16[256,512,16]{2,1,0:T(8,128)(2,1)} %get-tuple-element.6) | data formatting | bytes 8388608
  433.2 6.0 convolution_bitcast_fusion.22
  439.2 4.7 fusion.8
  445.0 1.8 fusion.9
  447.2 1.8 fusion.10
  450.0 1.8 fusion.11
  453.0 1.8 fusion.12
  456.0 1.8 fusion.13
  459.0 2.6 fusion.15
  461.8 39.7 %all-reduce.5.cloned.1.call-done = f32[256,384]{0,1:T(8,128)} async-done(((f32[256,384]{0,1:T(8,128)}), f32[256,384]{0,1:T(8,128)}) %all-reduce.5.cloned.1.call-update) | async-done | bytes 393232 | tf_op jit(solution)/shard_map/psum | solution.py:57
  501.5 1.8 fusion.152
  504.2 2.4 constant_dynamic-update-slice_fusion.240
  519.4 2.1 constant_dynamic-update-slice_fusion.224
  533.4 1.8 constant_dynamic-update-slice_fusion.208
  572.1 7.9 convolution_bitcast_fusion.7
  579.9 10.6 %fusion.7 = f32[1408,512]{1,0:T(8,128)} fusion(f32[1408,512]{1,0:T(8,128)} %convolution_bitcast_fusion.7, bf16[256,16,1408]{0,2,1:T(8,128)(2,1)} %get-tuple-element.306, bf16[256,512,16]{1,0,2:T(8,128)(2,1)S(1)} %copy-done.21), kind=kOutput, calls=%fused_computation.142 | convolution fusion | flops 5906300928 | bytes 21495808 | tf_op jit(solution)/shard_map/hlk,hkm->lm/dot_general | solution.py:47
  590.5 10.8 %fusion.6 = f32[1408,512]{1,0:T(8,128)} fusion(f32[1408,512]{1,0:T(8,128)} %fusion.7, bf16[256,16,1408]{0,2,1:T(8,128)(2,1)} %copy-done.28, bf16[256,512,16]{1,0,2:T(8,128)(2,1)S(1)} %copy-done.16), kind=kOutput, calls=%fused_computation.140 | convolution fusion | flops 5906300928 | bytes 21495808 | tf_op jit(solution)/shard_map/hlk,hkm->lm/dot_general | solution.py:47
  601.4 8.9 %fusion.5 = f32[1408,512]{1,0:T(8,128)} fusion(f32[1408,512]{1,0:T(8,128)} %fusion.6, bf16[256,16,1408]{0,2,1:T(8,128)(2,1)S(1)} %bitcast.1687, bf16[256,512,16]{1,0,2:T(8,128)(2,1)S(1)} %copy-done.13), kind=kOutput, calls=%fused_computation.138 | convolution fusion | flops 5906300928 | bytes 21495808 | tf_op jit(solution)/shard_map/hlk,hkm->lm/dot_general | solution.py:47
  610.3 10.6 %fusion.4 = f32[1408,512]{1,0:T(8,128)} fusion(f32[1408,512]{1,0:T(8,128)} %fusion.5, bf16[256,16,1408]{0,2,1:T(8,128)(2,1)} %get-tuple-element.294, bf16[256,512,16]{1,0,2:T(8,128)(2,1)S(1)} %copy-done.10), kind=kOutput, calls=%fused_computation.136 | convolution fusion | flops 5906300928 | bytes 21495808 | tf_op jit(solution)/shard_map/hlk,hkm->lm/dot_general | solution.py:47
  620.9 10.6 %fusion.3 = f32[1408,512]{1,0:T(8,128)} fusion(f32[1408,512]{1,0:T(8,128)} %fusion.4, bf16[256,16,1408]{0,2,1:T(8,128)(2,1)} %get-tuple-element.288, bf16[256,512,16]{1,0,2:T(8,128)(2,1)S(1)} %copy-done.7), kind=kOutput, calls=%fused_computation.134 | convolution fusion | flops 5906300928 | bytes 21495808 | tf_op jit(solution)/shard_map/hlk,hkm->lm/dot_general | solution.py:47
  631.6 8.9 %fusion.2 = f32[1408,512]{1,0:T(8,128)} fusion(f32[1408,512]{1,0:T(8,128)} %fusion.3, bf16[256,16,1408]{0,2,1:T(8,128)(2,1)S(1)} %bitcast.1689, bf16[256,512,16]{1,0,2:T(8,128)(2,1)S(1)} %copy-done.4), kind=kOutput, calls=%fused_computation.132 | convolution fusion | flops 5906300928 | bytes 21495808 | tf_op jit(solution)/shard_map/hlk,hkm->lm/dot_general | solution.py:47
  640.5 8.7 %fusion.1 = f32[512,1408]{0,1:T(8,128)} fusion(f32[1408,512]{1,0:T(8,128)} %fusion.2, bf16[256,16,1408]{0,2,1:T(8,128)(2,1)S(1)} %get-tuple-element.271, bf16[256,512,16]{1,0,2:T(8,128)(2,1)S(1)} %copy-done.24), kind=kOutput, calls=%fused_computation.130 | convolution fusion | flops 5906300928 | bytes 21495808 | tf_op jit(solution)/shard_map/hlk,hkm->lm/dot_general | solution.py:47
  649.6 66.4 %all-reduce.7.cloned.1.call-done = f32[512,1408]{0,1:T(8,128)} async-done(((f32[512,1408]{0,1:T(8,128)}), f32[512,1408]{0,1:T(8,128)}) %all-reduce.7.cloned.1.call-update) | async-done | bytes 2883600 | tf_op jit(solution)/shard_map/psum | solution.py:60
  716.0 4.0 fusion.154
  736.6 2.7 copy-done.31
  741.6 2.6 copy-done.30
  744.2 4.7 convolution_bitcast_fusion.14
  749.0 4.8 fusion.16
  753.7 4.7 fusion.17
  758.5 4.7 fusion.18
  763.3 1.8 fusion.19
  765.5 1.8 fusion.20
  767.4 2.1 fusion.21
  769.5 2.6 fusion.23
  772.1 37.2 %all-reduce.9.cloned.1.call-done = f32[256,384]{0,1:T(8,128)} async-done(((f32[256,384]{0,1:T(8,128)}), f32[256,384]{0,1:T(8,128)}) %all-reduce.9.cloned.1.call-update) | async-done | bytes 393232 | tf_op jit(solution)/shard_map/psum | solution.py:64
  809.3 1.7 multiply_reduce_fusion.1
  811.0 10.9 %psum.37 = f32[]{:T(128)} all-reduce(f32[]{:T(128)} %get-tuple-element.15), channel_id=1, replica_groups=mesh['hot'=8,'load'=4] {'load'}, use_global_device_ids=true, to_apply=%region_3.4 | all-reduce | flops 1 | bytes 8 | tf_op jit(solution)/shard_map/psum | solution.py:62
  821.9 12.4 %psum.39 = f32[]{:T(128)} all-reduce(f32[]{:T(128)} %multiply_reduce_fusion.1), channel_id=1, replica_groups=mesh['hot'=8,'load'=4] {'hot'}, use_global_device_ids=true, to_apply=%region_6.7 | all-reduce | flops 1 | bytes 8 | tf_op jit(solution)/shard_map/psum | solution.py:66
  837.6 3.9 multiply_add_fusion
  841.5 3.4 copy.143
  (226 shorter events, 93.1 us)
Async XLA Ops:
  7.2 494.3 %all-reduce.5.cloned.1.call-start = ((), (), s32[]{:S(2)}) async-start(), calls=%async_computation | async-start | bytes 786432 | tf_op jit(solution)/shard_map/psum | solution.py:57
  8.9 182.0 %copy-start = (bf16[512,1408]{0,1:T(8,128)(2,1)}, bf16[512,1408]{0,1:T(8,128)(2,1)S(1)}, u32[]{:S(2)}) copy-start(bf16[512,1408]{0,1:T(8,128)(2,1)S(1)} %copy.5) | copy-start | bytes 4325380
  352.4 27.0 %copy-start.1 = (bf16[512,1408]{0,1:T(8,128)(2,1)S(1)}, bf16[512,1408]{0,1:T(8,128)(2,1)}, u32[]{:S(2)}) copy-start(bf16[512,1408]{0,1:T(8,128)(2,1)} %copy-done) | copy-start | bytes 4325380
  403.1 2.6 copy-start.29
  433.2 6.0 copy-start.18
  433.2 13.7 %slice-start.14 = ((s8[6291456]{0:T(1024)(128)(4,1)}), s8[4194304]{0:T(1024)(128)(4,1)S(1)}, s32[]{:S(2)}) async-start(s8[6291456]{0:T(1024)(128)(4,1)} %bitcast.1698), calls=%async_computation.17 | async-start | bytes 8388608
  439.2 4.8 copy-start.15
  439.2 5.9 copy-start.32
  439.2 7.7 slice-start.15
  439.2 9.9 %slice-start.12 = ((s8[6291456]{0:T(1024)(128)(4,1)}), s8[4194304]{0:T(1024)(128)(4,1)S(1)}, s32[]{:S(2)}) async-start(s8[6291456]{0:T(1024)(128)(4,1)} %bitcast.1696), calls=%async_computation.15 | async-start | bytes 8388608
  444.0 3.2 copy-start.12
  445.0 4.0 slice-start.13
  445.0 7.3 slice-start.10
  446.9 3.1 copy-start.9
  447.2 5.8 slice-start.11
  447.2 7.7 slice-start.8
  449.0 4.0 copy-start.6
  450.0 4.9 slice-start.9
  451.8 4.2 copy-start.3
  453.0 4.8 slice-start.6
  454.8 3.6 copy-start.23
  454.8 4.1 slice-start.7
  459.0 2.6 copy-start.27
  461.6 254.4 %all-reduce.7.cloned.1.call-start = ((), (), s32[]{:S(2)}) async-start(), calls=%async_computation.1 | async-start | bytes 5767168 | tf_op jit(solution)/shard_map/psum | solution.py:60
  560.9 5.1 copy-start.28
  566.9 5.1 copy-start.19
  572.0 7.9 copy-start.21
  579.9 10.6 %copy-start.16 = (bf16[256,512,16]{1,0,2:T(8,128)(2,1)S(1)}, bf16[256,512,16]{1,0,2:T(8,128)(2,1)}, u32[]{:S(2)}) copy-start(bf16[256,512,16]{1,0,2:T(8,128)(2,1)} %copy.147) | copy-start | bytes 12582916
  579.9 21.4 %slice-start = ((s8[11534336]{0:T(1024)(128)(4,1)}), s8[4194304]{0:T(1024)(128)(4,1)S(1)}, s32[]{:S(2)}) async-start(s8[11534336]{0:T(1024)(128)(4,1)} %bitcast.1686), calls=%async_computation.3 | async-start | bytes 8388608
  579.9 21.4 %slice-start.1 = ((s8[11534336]{0:T(1024)(128)(4,1)}), s8[4194304]{0:T(1024)(128)(4,1)S(1)}, s32[]{:S(2)}) async-start(s8[11534336]{0:T(1024)(128)(4,1)} %bitcast.1686), calls=%async_computation.4 | async-start | bytes 8388608
  590.5 10.8 %copy-start.13 = (bf16[256,512,16]{1,0,2:T(8,128)(2,1)S(1)}, bf16[256,512,16]{1,0,2:T(8,128)(2,1)}, u32[]{:S(2)}) copy-start(bf16[256,512,16]{1,0,2:T(8,128)(2,1)} %copy.148) | copy-start | bytes 12582916
  590.5 10.8 %slice-start.2 = ((s8[11534336]{0:T(1024)(128)(4,1)}), s8[3145728]{0:T(1024)(128)(4,1)S(1)}, s32[]{:S(2)}) async-start(s8[11534336]{0:T(1024)(128)(4,1)} %bitcast.1686), calls=%async_computation.5 | async-start | bytes 6291456
  601.4 8.9 %copy-start.10 = (bf16[256,512,16]{1,0,2:T(8,128)(2,1)S(1)}, bf16[256,512,16]{1,0,2:T(8,128)(2,1)}, u32[]{:S(2)}) copy-start(bf16[256,512,16]{1,0,2:T(8,128)(2,1)} %copy.149) | copy-start | bytes 12582916
  610.3 10.6 %copy-start.7 = (bf16[256,512,16]{1,0,2:T(8,128)(2,1)S(1)}, bf16[256,512,16]{1,0,2:T(8,128)(2,1)}, u32[]{:S(2)}) copy-start(bf16[256,512,16]{1,0,2:T(8,128)(2,1)} %copy.150) | copy-start | bytes 12582916
  610.3 21.2 %slice-start.3 = ((s8[11534336]{0:T(1024)(128)(4,1)}), s8[4194304]{0:T(1024)(128)(4,1)S(1)}, s32[]{:S(2)}) async-start(s8[11534336]{0:T(1024)(128)(4,1)} %bitcast.1688), calls=%async_computation.6 | async-start | bytes 8388608
  610.3 21.2 %slice-start.4 = ((s8[11534336]{0:T(1024)(128)(4,1)}), s8[4194304]{0:T(1024)(128)(4,1)S(1)}, s32[]{:S(2)}) async-start(s8[11534336]{0:T(1024)(128)(4,1)} %bitcast.1688), calls=%async_computation.7 | async-start | bytes 8388608
  620.9 10.6 %copy-start.4 = (bf16[256,512,16]{1,0,2:T(8,128)(2,1)S(1)}, bf16[256,512,16]{1,0,2:T(8,128)(2,1)}, u32[]{:S(2)}) copy-start(bf16[256,512,16]{1,0,2:T(8,128)(2,1)} %copy.151) | copy-start | bytes 12582916
  620.9 10.6 %slice-start.5 = ((s8[11534336]{0:T(1024)(128)(4,1)}), s8[3145728]{0:T(1024)(128)(4,1)S(1)}, s32[]{:S(2)}) async-start(s8[11534336]{0:T(1024)(128)(4,1)} %bitcast.1688), calls=%async_computation.8 | async-start | bytes 6291456
  631.6 8.9 %copy-start.24 = (bf16[256,512,16]{1,0,2:T(8,128)(2,1)S(1)}, bf16[256,512,16]{1,0,2:T(8,128)(2,1)}, u32[]{:S(2)}) copy-start(bf16[256,512,16]{1,0,2:T(8,128)(2,1)} %copy.152) | copy-start | bytes 12582916
  649.3 160.0 %all-reduce.9.cloned.1.call-start = ((), (), s32[]{:S(2)}) async-start(), calls=%async_computation.2 | async-start | bytes 786432 | tf_op jit(solution)/shard_map/psum | solution.py:64
  736.6 2.7 copy-start.31
  739.3 4.9 copy-start.22
  741.6 2.6 copy-start.30
  744.2 4.8 copy-start.20
  748.9 4.8 copy-start.17
  753.7 4.8 copy-start.14
  758.5 4.8 copy-start.11
  763.3 2.2 copy-start.8
  765.1 2.3 copy-start.5
  767.3 2.2 copy-start.25
  769.5 66.1 %copy-start.26 = (f32[256,384]{0,1:T(8,128)S(1)}, f32[256,384]{0,1:T(8,128)}, u32[]{:S(2)}) copy-start(f32[256,384]{0,1:T(8,128)} %get-tuple-element.5) | copy-start | bytes 1179652
  769.5 68.1 %copy-start.2 = (bf16[512,1408]{0,1:T(8,128)(2,1)S(1)}, bf16[512,1408]{0,1:T(8,128)(2,1)}, u32[]{:S(2)}) copy-start(bf16[512,1408]{0,1:T(8,128)(2,1)} %copy-done) | copy-start | bytes 4325380
Sparse Core Ops, SparseCore 0:
  461.7 39.7 all-reduce.4
  649.4 66.5 all-reduce.6
  772.2 36.9 all-reduce.8
where the time goes:
time: 865 us; the launch traced here: 852 us
  local copies, waits for them, and re-layouts  529 us (61%)
  waiting for transfers between devices  143 us (17%)
  matrix products  127 us (15%)
  blocking collectives  23.3 us (3%)
  between operations  16.4 us (2%)
  other arithmetic  12.5 us (1%)
    unnamed x232, local copies, waits for them, and re-layouts  337 us
    slice x1, local copies, waits for them, and re-layouts, strain_product(): response[:, :, first_tap:first_tap + tap_span]  180 us
    dot_general x8, matrix products, load_product(): jnp.einsum('hlk,hkm->lm', response[:, :, first_tap:first_tap + tap_span],...  77 us
    psum x1, waiting for transfers between devices, body(): gradient = lax.psum(load_product(response, residual_b), 'hot')  66.4 us
    dot_general x16, matrix products, strain_product(): jnp.einsum('hlk,lkm->hm', response[:, :, first_tap:first_tap + tap_span],...  49.6 us
    psum x1, waiting for transfers between devices, body(): strains = lax.psum(strain_product(response, forces), 'load')  39.7 us
    psum x1, waiting for transfers between devices, body(): image_sum = lax.psum(strain_product(response, gradient_b), 'load')  37.2 us
  transfers between devices with their start and end apart: 3, of which 3 were waited for; matrix products, arithmetic and copies ran while one was open for 0% of the time, Pallas kernels for 0%

commit v1 on v0

v1 whole, which is shorter than its diff:
```python
import functools

import jax
import jax.numpy as jnp
from jax import lax
from jax.experimental import pallas as pl
from jax.experimental.pallas import tpu as pltpu
from jax.sharding import PartitionSpec as P

TAPS = 128
SEG = 48
CASES = 8
HIST = 128
STEPS = 176
COLS = STEPS * CASES
SEG_COLS = SEG * CASES
MIB = 1 << 20

STEP_TAPS = 8
GROUP = 4
WINDOW = -(-(SEG_COLS + (GROUP - 1) * CASES) // 16) * 16


def tap_major_kernel(hots, in_ref, out_ref, held):
    lanes = held.shape[2]
    for part in range(held.shape[0]):
        loads = slice(part * lanes, (part + 1) * lanes)
        for h in range(hots):
            held[part, pl.ds(h, TAPS, stride=hots), :] = in_ref[h, loads, :].T.astype(jnp.float32)
        out_ref[:, :, loads] = held[part].astype(jnp.bfloat16).reshape(TAPS, hots, lanes)


def tap_major(response):
    hots, loads, taps = response.shape
    block = 16
    return pl.pallas_call(
        functools.partial(tap_major_kernel, block),
        grid=(hots // block,),
        in_specs=[pl.BlockSpec((block, loads, taps), lambda i: (i, 0, 0))],
        out_specs=pl.BlockSpec((taps, block, loads), lambda i: (0, i, 0)),
        out_shape=jax.ShapeDtypeStruct((taps, hots, loads), response.dtype),
        scratch_shapes=[pltpu.VMEM((loads // 128, taps * block, 128), jnp.float32)],
        compiler_params=pltpu.CompilerParams(vmem_limit_bytes=40 * MIB),
        cost_estimate=pl.CostEstimate(
            flops=0, bytes_accessed=4 * response.size, transcendentals=0
        ),
        name="tap_major",
    )(response)


def strain_kernel(even_ref, odd_ref, tile_ref, out_ref):
    step = pl.program_id(0)

    @pl.when(step == 0)
    def _():
        out_ref[...] = jnp.zeros_like(out_ref)

    total = out_ref[...]
    for i in range(STEP_TAPS):
        parity = (HIST - i) % 2
        signal_ref = odd_ref if parity else even_ref
        first = (HIST - i - parity) * CASES - step * (STEP_TAPS * CASES)
        rows = pl.ds(pl.multiple_of(first, 16), SEG_COLS)
        total += lax.dot_general(
            signal_ref[rows, :],
            tile_ref[i],
            (((1,), (1,)), ((), ())),
            preferred_element_type=jnp.float32,
        )
    out_ref[...] = total


def strain_product(tiles, signal):
    taps, hots, loads = tiles.shape
    odd = jnp.concatenate([signal[CASES:], signal[:CASES]])
    whole = pl.BlockSpec((COLS, loads), lambda i: (0, 0))
    return pl.pallas_call(
        strain_kernel,
        grid=(taps // STEP_TAPS,),
        in_specs=[whole, whole, pl.BlockSpec((STEP_TAPS, hots, loads), lambda i: (i, 0, 0))],
        out_specs=pl.BlockSpec((SEG_COLS, hots), lambda i: (0, 0)),
        out_shape=jax.ShapeDtypeStruct((SEG_COLS, hots), jnp.float32),
        compiler_params=pltpu.CompilerParams(vmem_limit_bytes=40 * MIB),
        cost_estimate=pl.CostEstimate(
            flops=2 * SEG_COLS * tiles.size, bytes_accessed=2 * tiles.size, transcendentals=0
        ),
        name="strain_product",
    )(signal, odd, tiles)


def gradient_kernel(hots, strains_ref, tile_ref, out_ref, held):
    step = pl.program_id(0)

    @pl.when(step == 0)
    def _():
        held[...] = jnp.zeros_like(held)

    for i in range(0, STEP_TAPS, GROUP):
        first = (HIST - i - (GROUP - 1)) * CASES - step * (STEP_TAPS * CASES)
        rows = pl.ds(pl.multiple_of(first, CASES), WINDOW)
        tile = tile_ref[i : i + GROUP].reshape(GROUP * hots, tile_ref.shape[2])
        held[rows, :] += jnp.dot(strains_ref[...], tile, preferred_element_type=jnp.float32)

    @pl.when(step == TAPS // STEP_TAPS - 1)
    def _():
        out_ref[...] = held[:COLS, :]


def load_product(tiles, strains):
    taps, hots, loads = tiles.shape
    stacked = jnp.concatenate(
        [
            jnp.pad(
                strains,
                (((GROUP - 1 - i) * CASES, WINDOW - SEG_COLS - (GROUP - 1 - i) * CASES), (0, 0)),
            )
            for i in range(GROUP)
        ],
        axis=1,
    )
    return pl.pallas_call(
        functools.partial(gradient_kernel, hots),
        grid=(taps // STEP_TAPS,),
        in_specs=[
            pl.BlockSpec((WINDOW, GROUP * hots), lambda i: (0, 0)),
            pl.BlockSpec((STEP_TAPS, hots, loads), lambda i: (i, 0, 0)),
        ],
        out_specs=pl.BlockSpec((COLS, loads), lambda i: (0, 0)),
        out_shape=jax.ShapeDtypeStruct((COLS, loads), jnp.float32),
        scratch_shapes=[pltpu.VMEM((COLS + 16, loads), jnp.float32)],
        compiler_params=pltpu.CompilerParams(vmem_limit_bytes=40 * MIB),
        cost_estimate=pl.CostEstimate(
            flops=2 * WINDOW * tiles.size, bytes_accessed=2 * tiles.size, transcendentals=0
        ),
        name="load_product",
    )(stacked, tiles)


def body(response, forces, measured):
    tiles = tap_major(response)
    strains = lax.psum(strain_product(tiles, forces.T), "load")
    residual = measured.T - strains
    gradient = lax.psum(load_product(tiles, residual.astype(jnp.bfloat16)), "hot")
    grad_total = lax.psum(jnp.sum(gradient * gradient), "load")
    image = lax.psum(strain_product(tiles, gradient.astype(jnp.bfloat16)), "load")
    image_total = lax.psum(jnp.sum(image * image), "hot")
    step_size = grad_total / image_total
    updated_forces = forces.astype(jnp.float32) + step_size * gradient.T
    return updated_forces, (residual - step_size * image).T


def solution(mesh):
    placed = (P("hot", "load", None), P("load", None), P("hot", None))
    return jax.shard_map(
        body,
        mesh=mesh,
        in_specs=placed,
        out_specs=(P("load", None), P("hot", None)),
        check_vma=False,
    )
```

time: 865 us -> 311 us (0.36); the launches traced: 852 us -> 309 us
  local copies, waits for them, and re-layouts: 529 us -> 7.91 us
  matrix products: 127 us -> 0 us
  Pallas kernels: 0 us -> 107 us
    unnamed x232 -> x10, local copies, waits for them, and re-layouts: 337 us -> 7.72 us
    slice x1 -> x4, local copies, waits for them, and re-layouts: 180 us -> 0.19 us  [strain_product(): odd = jnp.concatenate([signal[CASES:], signal[:CASES]])]
    dot_general x24 -> x0, matrix products: 127 us -> none  [the longest x8 77 us: load_product(): jnp.einsum('hlk,hkm->lm', response[:, :, first_tap:first_tap + tap_span],...]
    pallas_call x0 -> x4, Pallas kernels: none -> 107 us  [the longest x2 46.8 us: strain_product(): pl.pallas_call(strain_kernel, grid=(taps // STEP_TAPS,), in_specs=[whole,...]
    another operation x10 -> x0, local copies, waits for them, and re-layouts: 12.3 us -> none  [the longest x8 11.1 us: load_product(): jnp.stack([padded[:, tap_index * CASES:tap_index * CASES + col_count] for...]
where the time goes in v1:
time: 311 us; the launch traced here: 309 us
  waiting for transfers between devices  144 us (46%)
  Pallas kernels  107 us (34%)
  blocking collectives  23.3 us (7%)
  between operations  15.2 us (5%)
  other arithmetic  11.9 us (4%)
  local copies, waits for them, and re-layouts  7.91 us (3%)
    psum x1, waiting for transfers between devices, body(): lax.psum(load_product(tiles, residual.astype(jnp.bfloat16)), 'hot')  66.7 us
    pallas_call x2, Pallas kernels, strain_product(): pl.pallas_call(strain_kernel, grid=(taps // STEP_TAPS,), in_specs=[whole,...  46.8 us
    psum x1, waiting for transfers between devices, body(): strains = lax.psum(strain_product(tiles, forces.T), 'load')  39.7 us
    psum x1, waiting for transfers between devices, body(): lax.psum(strain_product(tiles, gradient.astype(jnp.bfloat16)), 'load')  37.2 us
    pallas_call x1, Pallas kernels, tap_major(): pl.pallas_call(functools.partial(tap_major_kernel, block), grid=(hots //...  36.9 us
    pallas_call x1, Pallas kernels, load_product(): pl.pallas_call(functools.partial(gradient_kernel, hots), grid=(taps // ST...  23.2 us
    psum x1, blocking collectives, body(): image_total = lax.psum(jnp.sum(image * image), 'hot')  12.4 us
    psum x1, blocking collectives, body(): grad_total = lax.psum(jnp.sum(gradient * gradient), 'load')  10.9 us
  transfers between devices with their start and end apart: 3, of which 3 were waited for; matrix products, arithmetic and copies ran while one was open for 0% of the time, Pallas kernels for 0%

profile of v1, /device:TPU:0, one launch (start us, length us, event | category | flops | bytes accessed | tf_op | source)
XLA Modules:
  0.0 309.0 jit_solution(16614413854318526946)
XLA Ops:
  7.2 0.0 all-reduce.8.cloned.1.call-start
  7.2 1.7 copy.5
  8.9 0.1 slice.16
  9.0 36.9 %tap_major.1.tile_ref = bf16[128,256,512]{2,1,0:T(8,128)(2,1)} custom-call(bf16[256,512,128]{2,1,0:T(8,128)(2,1)} %in_ref.1), custom_call_target="tpu_custom_call" | custom-call | bytes 67108864 | tf_op jit(solution)/shard_map/tap_major/pallas_call | solution.py:36
  45.9 0.1 pad_maximum_fusion.odd_ref
  46.0 0.0 copy-start.2
  46.1 23.4 %strain_product.2 = f32[384,256]{1,0:T(8,128)} custom-call(bf16[1408,512]{1,0:T(8,128)(2,1)S(1)} %bitcast.13, bf16[1408,512]{1,0:T(8,128)(2,1)S(1)} %pad_maximum_fusion.odd_ref, bf16[128,256,512]{2,1,0:T(8,128)(2,1)} %tap_major.1.tile_ref), custom_call_target="tpu_custom_call" | custom-call | flops 12884901888 | bytes 33554432 | tf_op jit(solution)/shard_map/strain_product/pallas_call | solution.py:77
  69.5 0.0 all-reduce.8.cloned.1.call-update
  69.5 0.0 all-reduce.10.cloned.1.call-start
  69.5 0.0 copy-done.2
  69.5 0.2 copy.6
  69.7 39.7 %all-reduce.8.cloned.1.call-done = f32[384,256]{1,0:T(8,128)} async-done(((f32[384,256]{1,0:T(8,128)}), f32[384,256]{1,0:T(8,128)}) %all-reduce.8.cloned.1.call-update) | async-done | bytes 393232 | tf_op jit(solution)/shard_map/psum | solution.py:141
  109.4 1.0 fusion.9
  110.4 0.1 fusion.7.strains_ref
  110.5 23.2 %load_product.1 = f32[1408,512]{1,0:T(8,128)S(1)} custom-call(bf16[416,1024]{1,0:T(8,128)(2,1)S(1)} %fusion.7.strains_ref, bf16[128,256,512]{2,1,0:T(8,128)(2,1)} %tap_major.1.tile_ref), custom_call_target="tpu_custom_call" | custom-call | flops 13958643712 | bytes 33554432 | tf_op jit(solution)/shard_map/load_product/pallas_call | solution.py:121
  133.8 0.0 copy-start
  133.8 1.6 copy-done
  135.3 0.0 all-reduce.10.cloned.1.call-update
  135.4 0.0 all-reduce.12.cloned.1.call-start
  135.4 66.7 %all-reduce.10.cloned.1.call-done = f32[1408,512]{1,0:T(8,128)} async-done(((f32[1408,512]{1,0:T(8,128)}), f32[1408,512]{1,0:T(8,128)}) %all-reduce.10.cloned.1.call-update) | async-done | bytes 2883600 | tf_op jit(solution)/shard_map/psum | solution.py:143
  202.1 4.0 %fusion.10 = (bf16[1408,512]{1,0:T(8,128)(2,1)S(1)}, f32[]{:T(128)}) fusion(f32[1408,512]{1,0:T(8,128)} %all-reduce.10.cloned.1.call-done), kind=kLoop, calls=%fused_computation.23 | loop fusion | flops 2162687 | bytes 4325380 | tf_op jit(solution)/shard_map/convert_element_type | solution.py:145
  206.1 0.1 slice.18
  206.2 0.1 pad_maximum_fusion.1.odd_ref
  206.3 0.0 copy-start.1
  206.3 23.4 %strain_product.3 = f32[384,256]{1,0:T(8,128)} custom-call(bf16[1408,512]{1,0:T(8,128)(2,1)S(1)} %get-tuple-element.4.even_ref, bf16[1408,512]{1,0:T(8,128)(2,1)S(1)} %pad_maximum_fusion.1.odd_ref, bf16[128,256,512]{2,1,0:T(8,128)(2,1)} %tap_major.1.tile_ref), custom_call_target="tpu_custom_call" | custom-call | flops 12884901888 | bytes 33554432 | tf_op jit(solution)/shard_map/strain_product/pallas_call | solution.py:77
  229.7 0.0 all-reduce.12.cloned.1.call-update
  229.8 37.2 %all-reduce.12.cloned.1.call-done = f32[384,256]{1,0:T(8,128)} async-done(((f32[384,256]{1,0:T(8,128)}), f32[384,256]{1,0:T(8,128)}) %all-reduce.12.cloned.1.call-update) | async-done | bytes 393232 | tf_op jit(solution)/shard_map/psum | solution.py:145
  266.9 1.7 multiply_reduce_fusion.1
  268.6 10.9 %psum.37 = f32[]{:T(128)} all-reduce(f32[]{:T(128)} %get-tuple-element.5), channel_id=1, replica_groups=mesh['hot'=8,'load'=4] {'load'}, use_global_device_ids=true, to_apply=%region_3.4 | all-reduce | flops 1 | bytes 8 | tf_op jit(solution)/shard_map/psum | solution.py:144
  279.5 12.4 %psum.39 = f32[]{:T(128)} all-reduce(f32[]{:T(128)} %multiply_reduce_fusion.1), channel_id=1, replica_groups=mesh['hot'=8,'load'=4] {'hot'}, use_global_device_ids=true, to_apply=%region_6.7 | all-reduce | flops 1 | bytes 8 | tf_op jit(solution)/shard_map/psum | solution.py:146
  293.3 0.0 copy-done.1
  293.3 1.1 subtract_bitcast_fusion
  294.3 0.9 copy.9
  295.3 3.9 %bitcast_add_fusion = f32[512,1408]{0,1:T(8,128)} fusion(f32[1408,512]{1,0:T(8,128)} %all-reduce.10.cloned.1.call-done, bf16[512,1408]{0,1:T(8,128)(2,1)S(1)} %copy.5, f32[]{:T(128)S(6)} %div.3), kind=kLoop, calls=%fused_computation | loop fusion | flops 2162688 | bytes 7208964 | tf_op jit(solution)/shard_map/add | solution.py:148
  299.1 3.4 %copy.8 = f32[512,1408]{1,0:T(8,128)} copy(f32[512,1408]{0,1:T(8,128)} %bitcast_add_fusion) | data formatting | bytes 5767168
  (2 shorter events, 0.0 us)
Async XLA Ops:
  7.2 102.2 %all-reduce.8.cloned.1.call-start = ((), (), s32[]{:S(2)}) async-start(), calls=%async_computation | async-start | bytes 786432 | tf_op jit(solution)/shard_map/psum | solution.py:141
  46.0 23.5 %copy-start.2 = (f32[256,384]{1,0:T(8,128)S(1)}, f32[256,384]{1,0:T(8,128)}, u32[]{:S(2)}) copy-start(f32[256,384]{1,0:T(8,128)} %param.5) | copy-start | bytes 1179652
  69.5 132.6 %all-reduce.10.cloned.1.call-start = ((), (), s32[]{:S(2)}) async-start(), calls=%async_computation.1 | async-start | bytes 5767168 | tf_op jit(solution)/shard_map/psum | solution.py:143
  133.8 1.6 copy-start
  135.4 131.6 %all-reduce.12.cloned.1.call-start = ((), (), s32[]{:S(2)}) async-start(), calls=%async_computation.2 | async-start | bytes 786432 | tf_op jit(solution)/shard_map/psum | solution.py:145
  206.3 86.9 %copy-start.1 = (f32[384,256]{1,0:T(8,128)S(1)}, f32[384,256]{1,0:T(8,128)}, u32[]{:S(2)}) copy-start(f32[384,256]{1,0:T(8,128)} %all-reduce.8.cloned.1.call-done) | copy-start | bytes 1179652
Sparse Core Ops, SparseCore 0:
  69.6 39.7 all-reduce.7
  135.5 66.5 all-reduce.9
  229.9 36.9 all-reduce.11

commit v2 on v1

--- a/solution.py
+++ b/solution.py
@@ -16,8 +16,9 @@
 SEG_COLS = SEG * CASES
 MIB = 1 << 20
 
-STEP_TAPS = 8
 GROUP = 4
+STREAMS = 4
+STEP_TAPS = GROUP * STREAMS
 WINDOW = -(-(SEG_COLS + (GROUP - 1) * CASES) // 16) * 16
 
 
@@ -48,7 +49,15 @@
     )(response)
 
 
-def strain_kernel(even_ref, odd_ref, tile_ref, out_ref):
+def tile_specs(hots, loads):
+    return [
+        pl.BlockSpec((GROUP, hots, loads), lambda i, part=part: (i * STREAMS + part, 0, 0))
+        for part in range(STREAMS)
+    ]
+
+
+def strain_kernel(even_ref, odd_ref, *refs):
+    *tile_refs, out_ref = refs
     step = pl.program_id(0)
 
     @pl.when(step == 0)
@@ -63,7 +72,7 @@
         rows = pl.ds(pl.multiple_of(first, 16), SEG_COLS)
         total += lax.dot_general(
             signal_ref[rows, :],
-            tile_ref[i],
+            tile_refs[i // GROUP][i % GROUP],
             (((1,), (1,)), ((), ())),
             preferred_element_type=jnp.float32,
         )
@@ -77,7 +86,7 @@
     return pl.pallas_call(
         strain_kernel,
         grid=(taps // STEP_TAPS,),
-        in_specs=[whole, whole, pl.BlockSpec((STEP_TAPS, hots, loads), lambda i: (i, 0, 0))],
+        in_specs=[whole, whole, *tile_specs(hots, loads)],
         out_specs=pl.BlockSpec((SEG_COLS, hots), lambda i: (0, 0)),
         out_shape=jax.ShapeDtypeStruct((SEG_COLS, hots), jnp.float32),
         compiler_params=pltpu.CompilerParams(vmem_limit_bytes=40 * MIB),
@@ -85,10 +94,11 @@
             flops=2 * SEG_COLS * tiles.size, bytes_accessed=2 * tiles.size, transcendentals=0
         ),
         name="strain_product",
-    )(signal, odd, tiles)
-
-
-def gradient_kernel(hots, strains_ref, tile_ref, out_ref, held):
+    )(signal, odd, *[tiles] * STREAMS)
+
+
+def gradient_kernel(hots, strains_ref, *refs):
+    *tile_refs, out_ref, held = refs
     step = pl.program_id(0)
 
     @pl.when(step == 0)
@@ -98,16 +108,18 @@
     for i in range(0, STEP_TAPS, GROUP):
         first = (HIST - i - (GROUP - 1)) * CASES - step * (STEP_TAPS * CASES)
         rows = pl.ds(pl.multiple_of(first, CASES), WINDOW)
-        tile = tile_ref[i : i + GROUP].reshape(GROUP * hots, tile_ref.shape[2])
+        tile_ref = tile_refs[i // GROUP]
+        tile = tile_ref[...].reshape(GROUP * hots, tile_ref.shape[2])
         held[rows, :] += jnp.dot(strains_ref[...], tile, preferred_element_type=jnp.float32)
 
     @pl.when(step == TAPS // STEP_TAPS - 1)
     def _():
-        out_ref[...] = held[:COLS, :]
-
-
-def load_product(tiles, strains):
+        out_ref[...] = held[: out_ref.shape[0], :]
+
+
+def load_product(tiles, strains, parts):
     taps, hots, loads = tiles.shape
+    rows = -(-COLS // (8 * parts)) * 8 * parts
     stacked = jnp.concatenate(
         [
             jnp.pad(
@@ -123,28 +135,230 @@
         grid=(taps // STEP_TAPS,),
         in_specs=[
             pl.BlockSpec((WINDOW, GROUP * hots), lambda i: (0, 0)),
-            pl.BlockSpec((STEP_TAPS, hots, loads), lambda i: (i, 0, 0)),
-        ],
-        out_specs=pl.BlockSpec((COLS, loads), lambda i: (0, 0)),
-        out_shape=jax.ShapeDtypeStruct((COLS, loads), jnp.float32),
-        scratch_shapes=[pltpu.VMEM((COLS + 16, loads), jnp.float32)],
+            *tile_specs(hots, loads),
+        ],
+        out_specs=pl.BlockSpec((rows, loads), lambda i: (0, 0)),
+        out_shape=jax.ShapeDtypeStruct((rows, loads), jnp.float32),
+        scratch_shapes=[pltpu.VMEM((max(rows, COLS + 16), loads), jnp.float32)],
         compiler_params=pltpu.CompilerParams(vmem_limit_bytes=40 * MIB),
         cost_estimate=pl.CostEstimate(
             flops=2 * WINDOW * tiles.size, bytes_accessed=2 * tiles.size, transcendentals=0
         ),
         name="load_product",
-    )(stacked, tiles)
-
-
-def body(response, forces, measured):
+    )(stacked, *[tiles] * STREAMS)
+
+
+def greet(peers):
+    barrier = pltpu.get_barrier_semaphore()
+    for peer in peers:
+        pl.semaphore_signal(
+            barrier, inc=1, device_id=peer, device_id_type=pl.DeviceIdType.MESH
+        )
+    pl.semaphore_wait(barrier, len(peers))
+
+
+def send(source, target, send_sem, recv_sem, peer):
+    copy = pltpu.make_async_remote_copy(
+        src_ref=source,
+        dst_ref=target,
+        send_sem=send_sem,
+        recv_sem=recv_sem,
+        device_id=peer,
+        device_id_type=pl.DeviceIdType.MESH,
+    )
+    copy.start()
+    return copy
+
+
+def other(axis, count, step):
+    return {axis: lax.rem(lax.axis_index(axis) + step, count)}
+
+
+def add_over_load(count, in_ref, out_ref, parts, sems):
+    me = lax.axis_index("load")
+    chunk = in_ref.shape[0] // count
+
+    def rows(index):
+        return pl.ds(pl.multiple_of(index * chunk, 8), chunk)
+
+    copies = []
+    for step in range(1, count):
+        peer = other("load", count, step)
+        copies.append(
+            send(
+                in_ref.at[rows(peer["load"])],
+                parts.at[step - 1],
+                sems.at[0, step - 1],
+                sems.at[1, step - 1],
+                peer,
+            )
+        )
+    total = in_ref[rows(me), :]
+    for step, copy in enumerate(copies):
+        copy.wait()
+        total += parts[step]
+    out_ref[rows(me), :] = total
+    copies = []
+    for step in range(1, count):
+        mine = out_ref.at[rows(me)]
+        peer = other("load", count, step)
+        copies.append(send(mine, mine, sems.at[2, step - 1], sems.at[3, step - 1], peer))
+    for copy in copies:
+        copy.wait()
+
+
+def load_sum_kernel(count, in_ref, out_ref, parts, sems):
+    greet([other("load", count, step) for step in range(1, count)])
+    add_over_load(count, in_ref, out_ref, parts, sems)
+
+
+def load_sum(terms, count):
+    rows, cols = terms.shape
+    return pl.pallas_call(
+        functools.partial(load_sum_kernel, count),
+        in_specs=[pl.BlockSpec(memory_space=pltpu.VMEM)],
+        out_specs=pl.BlockSpec(memory_space=pltpu.VMEM),
+        out_shape=jax.ShapeDtypeStruct(terms.shape, terms.dtype),
+        scratch_shapes=[
+            pltpu.VMEM((count - 1, rows // count, cols), jnp.float32),
+            pltpu.SemaphoreType.DMA((4, count - 1)),
+        ],
+        compiler_params=pltpu.CompilerParams(
+            collective_id=0, has_side_effects=True, vmem_limit_bytes=40 * MIB
+        ),
+        name="load_sum",
+    )(terms)
+
+
+def image_sum_kernel(
+    loads, hots, in_ref, norm_ref, out_ref, step_ref, parts, load_norms, hot_norms, sems, load_sems, hot_sems
+):
+    load, hot = lax.axis_index("load"), lax.axis_index("hot")
+    load_peers = [other("load", loads, step) for step in range(1, loads)]
+    hot_peers = [other("hot", hots, step) for step in range(1, hots)]
+    greet(load_peers + hot_peers)
+
+    load_norms[load] = norm_ref[...]
+    copies = []
+    for i, peer in enumerate(load_peers):
+        mine = load_norms.at[load]
+        copies.append(send(mine, mine, load_sems.at[0, i], load_sems.at[1, i], peer))
+    add_over_load(loads, in_ref, out_ref, parts, sems)
+    image = out_ref[...]
+    hot_norms[hot] = jnp.full(hot_norms.shape[1:], jnp.sum(image * image))
+    for i, peer in enumerate(hot_peers):
+        mine = hot_norms.at[hot]
+        copies.append(send(mine, mine, hot_sems.at[0, i], hot_sems.at[1, i], peer))
+    for copy in copies:
+        copy.wait()
+    step_ref[...] = jnp.sum(load_norms[...], axis=0) / jnp.sum(hot_norms[...], axis=0)
+
+
+def image_sum(terms, norm, loads, hots):
+    rows, cols = terms.shape
+    tile = (8, 128)
+    vmem = pl.BlockSpec(memory_space=pltpu.VMEM)
+    image, step = pl.pallas_call(
+        functools.partial(image_sum_kernel, loads, hots),
+        in_specs=[vmem, vmem],
+        out_specs=[vmem, vmem],
+        out_shape=[
+            jax.ShapeDtypeStruct(terms.shape, jnp.float32),
+            jax.ShapeDtypeStruct(tile, jnp.float32),
+        ],
+        scratch_shapes=[
+            pltpu.VMEM((loads - 1, rows // loads, cols), jnp.float32),
+            pltpu.VMEM((loads,) + tile, jnp.float32),
+            pltpu.VMEM((hots,) + tile, jnp.float32),
+            pltpu.SemaphoreType.DMA((4, loads - 1)),
+            pltpu.SemaphoreType.DMA((2, loads - 1)),
+            pltpu.SemaphoreType.DMA((2, hots - 1)),
+        ],
+        compiler_params=pltpu.CompilerParams(
+            collective_id=1, has_side_effects=True, vmem_limit_bytes=40 * MIB
+        ),
+        name="image_sum",
+    )(terms, jnp.broadcast_to(norm, tile))
+    return image, step[0, 0]
+
+
+def hot_sum_kernel(count, in_ref, out_ref, pair, held, parts, pair_sems, part_sems, gather_sems, swap_sems):
+    me = lax.axis_index("hot")
+    core, chip, chips = lax.rem(me, 2), me // 2, count // 2
+    chunk = in_ref.shape[0] // count
+    partner = {"hot": me + 1 - 2 * core}
+    order = [lax.rem(chip + step, chips) for step in range(1, chips + 1)]
+    peers = [{"hot": order[i] * 2 + core} for i in range(chips - 1)]
+
+    def rows(of_core, of_chip):
+        return pl.ds(pl.multiple_of((of_core * chips + of_chip) * chunk, 8), chunk)
+
+    greet([partner] + peers)
+    halves = []
+    for i, at in enumerate(order):
+        source = in_ref.at[rows(1 - core, at)]
+        halves.append(send(source, pair.at[i], pair_sems.at[0, i], pair_sems.at[1, i], partner))
+    copies = []
+    for i, at in enumerate(order):
+        halves[i].wait()
+        held[i] = in_ref[rows(core, at), :] + pair[i]
+        if i < chips - 1:
+            copies.append(
+                send(held.at[i], parts.at[i], part_sems.at[0, i], part_sems.at[1, i], peers[i])
+            )
+    total = held[chips - 1]
+    for i, copy in enumerate(copies):
+        copy.wait()
+        total += parts[i]
+    out_ref[rows(core, chip), :] = total
+
+    mine = out_ref.at[rows(core, chip)]
+    copies = [
+        send(mine, mine, gather_sems.at[0, i], gather_sems.at[1, i], peers[i])
+        for i in range(chips - 1)
+    ]
+    swaps = [send(mine, mine, swap_sems.at[0, 0], swap_sems.at[1, 0], partner)]
+    for i, copy in enumerate(copies):
+        copy.wait()
+        came = out_ref.at[rows(core, lax.rem(chip + chips - 1 - i, chips))]
+        swaps.append(send(came, came, swap_sems.at[0, i + 1], swap_sems.at[1, i + 1], partner))
+    for copy in swaps:
+        copy.wait()
+
+
+def hot_sum(terms, count):
+    rows, cols = terms.shape
+    chunk, chips = rows // count, count // 2
+    return pl.pallas_call(
+        functools.partial(hot_sum_kernel, count),
+        in_specs=[pl.BlockSpec(memory_space=pltpu.VMEM)],
+        out_specs=pl.BlockSpec(memory_space=pltpu.VMEM),
+        out_shape=jax.ShapeDtypeStruct(terms.shape, terms.dtype),
+        scratch_shapes=[
+            pltpu.VMEM((chips, chunk, cols), jnp.float32),
+            pltpu.VMEM((chips, chunk, cols), jnp.float32),
+            pltpu.VMEM((chips - 1, chunk, cols), jnp.float32),
+            pltpu.SemaphoreType.DMA((2, chips)),
+            pltpu.SemaphoreType.DMA((2, chips - 1)),
+            pltpu.SemaphoreType.DMA((2, chips - 1)),
+            pltpu.SemaphoreType.DMA((2, chips)),
+        ],
+        compiler_params=pltpu.CompilerParams(
+            collective_id=2, has_side_effects=True, vmem_limit_bytes=40 * MIB
+        ),
+        name="hot_sum",
+    )(terms)
+
+
+def body(loads, hots, response, forces, measured):
     tiles = tap_major(response)
-    strains = lax.psum(strain_product(tiles, forces.T), "load")
+    strains = load_sum(strain_product(tiles, forces.T), loads)
     residual = measured.T - strains
-    gradient = lax.psum(load_product(tiles, residual.astype(jnp.bfloat16)), "hot")
-    grad_total = lax.psum(jnp.sum(gradient * gradient), "load")
-    image = lax.psum(strain_product(tiles, gradient.astype(jnp.bfloat16)), "load")
-    image_total = lax.psum(jnp.sum(image * image), "hot")
-    step_size = grad_total / image_total
+    padded = hot_sum(load_product(tiles, residual.astype(jnp.bfloat16), hots), hots)
+    gradient = padded[:COLS]
+    norm = jnp.sum(gradient * gradient)
+    terms = strain_product(tiles, gradient.astype(jnp.bfloat16))
+    image, step_size = image_sum(terms, norm, loads, hots)
     updated_forces = forces.astype(jnp.float32) + step_size * gradient.T
     return updated_forces, (residual - step_size * image).T
 
@@ -152,7 +366,7 @@
 def solution(mesh):
     placed = (P("hot", "load", None), P("load", None), P("hot", None))
     return jax.shard_map(
-        body,
+        functools.partial(body, mesh.shape["load"], mesh.shape["hot"]),
         mesh=mesh,
         in_specs=placed,
         out_specs=(P("load", None), P("hot", None)),

time: 311 us -> 199 us (0.64)
  waiting for transfers between devices: 144 us -> 0 us
  Pallas kernels: 107 us -> 181 us
  blocking collectives: 23.3 us -> 0 us
  between operations: 15.2 us -> 0.8 us
  other arithmetic: 11.9 us -> 7 us
    psum x3 -> x0, waiting for transfers between devices: 144 us -> none  [the longest x1 66.7 us: body(): lax.psum(load_product(tiles, residual.astype(jnp.bfloat16)), 'hot')]
    pallas_call x0 -> x3, Pallas kernels: none -> 88.5 us  [the longest x1 41.1 us: hot_sum(): pl.pallas_call(functools.partial(hot_sum_kernel, count), in_specs=[pl.Blo...]
    psum x2 -> x0, blocking collectives: 23.3 us -> none  [the longest x1 12.4 us: body(): image_total = lax.psum(jnp.sum(image * image), 'hot')]
    pallas_call x2, Pallas kernels: 46.8 us -> 36.3 us  [strain_product(): pl.pallas_call(strain_kernel, grid=(taps // STEP_TAPS,), in_specs=[whole,...]
    pallas_call x1, Pallas kernels: 23.2 us -> 18.9 us  [load_product(): pl.pallas_call(functools.partial(gradient_kernel, hots), grid=(taps // ST...]
    convert_element_type x1 -> x0, other arithmetic: 4.03 us -> none  [body(): gradient.astype(jnp.bfloat16)]
    unnamed x10 -> x12, local copies, waits for them, and re-layouts: 7.72 us -> 7.75 us
  transfers between devices with their start and end apart: 3 -> 0, of which waited for: 3 -> 0; matrix products, arithmetic and copies ran while one was open for 0% -> 0% of each run, Pallas kernels for 0% -> 0%
where the time goes in v2:
time: 199 us; the launch traced here: 198 us
  Pallas kernels  181 us (91%)
  local copies, waits for them, and re-layouts  9.01 us (5%)
  other arithmetic  7 us (4%)
    pallas_call x1, Pallas kernels, hot_sum(): pl.pallas_call(functools.partial(hot_sum_kernel, count), in_specs=[pl.Blo...  41.1 us
    pallas_call x1, Pallas kernels, tap_major(): pl.pallas_call(functools.partial(tap_major_kernel, block), grid=(hots //...  37.2 us
    pallas_call x2, Pallas kernels, strain_product(): pl.pallas_call(strain_kernel, grid=(taps // STEP_TAPS,), in_specs=[whole,...  36.3 us
    pallas_call x1, Pallas kernels, image_sum(): pl.pallas_call(functools.partial(image_sum_kernel, loads, hots), in_specs...  25.2 us
    pallas_call x1, Pallas kernels, load_sum(): pl.pallas_call(functools.partial(load_sum_kernel, count), in_specs=[pl.Bl...  22.3 us
    pallas_call x1, Pallas kernels, load_product(): pl.pallas_call(functools.partial(gradient_kernel, hots), grid=(taps // ST...  18.9 us
    unnamed x12, local copies, waits for them, and re-layouts  7.75 us

profile of v2, /device:TPU:0, one launch (start us, length us, event | category | flops | bytes accessed | tf_op | source)
XLA Modules:
  0.0 197.8 jit_solution(15280083040522301592)
XLA Ops:
  0.6 1.7 copy.5
  2.3 0.0 copy-start
  2.3 0.1 slice.20
  2.4 0.1 pad_maximum_fusion.odd_ref
  2.5 37.2 %tap_major.1.refs_0_.refs_1_.refs_2_.refs_3_ = bf16[128,256,512]{2,1,0:T(8,128)(2,1)} custom-call(bf16[256,512,128]{2,1,0:T(8,128)(2,1)} %in_ref.1), custom_call_target="tpu_custom_call" | custom-call | bytes 67108864 | tf_op jit(solution)/shard_map/tap_major/pallas_call | solution.py:37
  39.7 0.0 copy-done
  39.8 0.0 copy-start.3
  39.8 18.2 %strain_product.2.in_ref = f32[384,256]{1,0:T(8,128)S(1)} custom-call(bf16[1408,512]{1,0:T(8,128)(2,1)S(1)} %bitcast.14, bf16[1408,512]{1,0:T(8,128)(2,1)S(1)} %pad_maximum_fusion.odd_ref, bf16[128,256,512]{2,1,0:T(8,128)(2,1)} %tap_major.1.refs_0_.refs_1_.refs_2_.refs_3_, bf16[128,256,512]{2,1,0:T(8,128)(2,1)} %tap_major.1.refs_0_.refs_1_.refs_2_.refs_3_, ...), custom_call_target="tpu_custom_call" | custom-call | flops 12884901888 | bytes 33554432 | tf_op jit(solution)/shard_map/strain_product/pallas_call | solution.py:86
  57.9 22.3 %load_sum.1 = f32[384,256]{1,0:T(8,128)S(1)} custom-call(f32[384,256]{1,0:T(8,128)S(1)} %strain_product.2.in_ref), custom_call_target="tpu_custom_call" | custom-call | tf_op jit(solution)/shard_map/load_sum/pallas_call | solution.py:217
  80.2 0.0 copy-done.3
  80.2 0.2 copy.6
  80.4 0.0 copy-start.1
  80.4 0.1 fusion.9
  80.5 0.1 fusion.7.strains_ref
  80.5 0.6 copy-done.1
  81.1 18.9 %load_product.1.in_ref = f32[1408,512]{1,0:T(8,128)S(1)} custom-call(bf16[416,1024]{1,0:T(8,128)(2,1)S(1)} %fusion.7.strains_ref, bf16[128,256,512]{2,1,0:T(8,128)(2,1)} %tap_major.1.refs_0_.refs_1_.refs_2_.refs_3_, bf16[128,256,512]{2,1,0:T(8,128)(2,1)} %tap_major.1.refs_0_.refs_1_.refs_2_.refs_3_, ...), custom_call_target="tpu_custom_call" | custom-call | flops 13958643712 | bytes 33554432 | tf_op jit(solution)/shard_map/load_product/pallas_call | solution.py:133
  100.0 41.1 %hot_sum.1 = f32[1408,512]{1,0:T(8,128)S(1)} custom-call(f32[1408,512]{1,0:T(8,128)S(1)} %load_product.1.in_ref), custom_call_target="tpu_custom_call" | custom-call | tf_op jit(solution)/shard_map/hot_sum/pallas_call | solution.py:332
  141.1 1.3 multiply_reduce_fusion
  142.4 0.1 slice.22
  142.6 0.1 pad_maximum_fusion.1.odd_ref
  142.7 0.0 copy-start.2
  142.7 18.2 %strain_product.3.in_ref = f32[384,256]{1,0:T(8,128)S(1)} custom-call(bf16[1408,512]{1,0:T(8,128)(2,1)S(1)} %get-tuple-element.9.even_ref, bf16[1408,512]{1,0:T(8,128)(2,1)S(1)} %pad_maximum_fusion.1.odd_ref, bf16[128,256,512]{2,1,0:T(8,128)(2,1)} %tap_major.1.refs_0_.refs_1_.refs_2_.refs_3_, ...), custom_call_target="tpu_custom_call" | custom-call | flops 12884901888 | bytes 33554432 | tf_op jit(solution)/shard_map/strain_product/pallas_call | solution.py:86
  160.8 0.6 broadcast_in_dim.3.norm_ref
  161.4 25.2 %image_sum.1 = (f32[384,256]{1,0:T(8,128)S(1)}, f32[8,128]{1,0:T(8,128)S(1)}) custom-call(f32[384,256]{1,0:T(8,128)S(1)} %strain_product.3.in_ref, f32[8,128]{1,0:T(8,128)S(1)} %broadcast_in_dim.3.norm_ref), custom_call_target="tpu_custom_call" | custom-call | tf_op jit(solution)/shard_map/image_sum/pallas_call | solution.py:261
  186.6 0.5 slice.19
  187.1 0.0 copy-done.2
  187.1 1.4 subtract_bitcast_fusion
  188.5 1.9 copy.9
  190.4 4.0 %bitcast_add_fusion = f32[512,1408]{0,1:T(8,128)} fusion(f32[1408,512]{1,0:T(8,128)S(1)} %hot_sum.1, bf16[512,1408]{0,1:T(8,128)(2,1)} %copy-done, f32[]{:T(128)} %bitcast.2), kind=kLoop, calls=%fused_computation | loop fusion | flops 2162688 | bytes 7208964 | tf_op jit(solution)/shard_map/add | solution.py:362
  194.4 3.4 %copy.8 = f32[512,1408]{1,0:T(8,128)} copy(f32[512,1408]{0,1:T(8,128)} %bitcast_add_fusion) | data formatting | bytes 5767168
  (2 shorter events, 0.0 us)
Async XLA Ops:
  2.3 37.4 %copy-start = (bf16[512,1408]{0,1:T(8,128)(2,1)}, bf16[512,1408]{0,1:T(8,128)(2,1)S(1)}, u32[]{:S(2)}) copy-start(bf16[512,1408]{0,1:T(8,128)(2,1)S(1)} %copy.5) | copy-start | bytes 4325380
  39.8 40.4 %copy-start.3 = (f32[256,384]{1,0:T(8,128)S(1)}, f32[256,384]{1,0:T(8,128)}, u32[]{:S(2)}) copy-start(f32[256,384]{1,0:T(8,128)} %param.5) | copy-start | bytes 1179652
  80.4 0.7 copy-start.1
  142.7 44.4 %copy-start.2 = (f32[256,384]{0,1:T(8,128)S(1)}, f32[256,384]{0,1:T(8,128)}, u32[]{:S(2)}) copy-start(f32[256,384]{0,1:T(8,128)} %copy-done.1) | copy-start | bytes 1179652

commit v3 on v2

--- a/solution.py
+++ b/solution.py
@@ -22,37 +22,49 @@
 WINDOW = -(-(SEG_COLS + (GROUP - 1) * CASES) // 16) * 16
 
 
-def tap_major_kernel(hots, in_ref, out_ref, held):
+def tap_major_kernel(hots, *refs):
+    in_refs, out_refs, held = refs[:STREAMS], refs[STREAMS:-1], refs[-1]
     lanes = held.shape[2]
+    each = hots // STREAMS
     for part in range(held.shape[0]):
         loads = slice(part * lanes, (part + 1) * lanes)
         for h in range(hots):
-            held[part, pl.ds(h, TAPS, stride=hots), :] = in_ref[h, loads, :].T.astype(jnp.float32)
-        out_ref[:, :, loads] = held[part].astype(jnp.bfloat16).reshape(TAPS, hots, lanes)
+            turned = in_refs[h // each][h % each, loads, :].T
+            held[part, pl.ds(h, TAPS, stride=hots), :] = turned.astype(jnp.float32)
+        turned = held[part].astype(jnp.bfloat16)
+        turned = turned.reshape(TAPS // STEP_TAPS, STREAMS, GROUP, hots, lanes)
+        for i, out_ref in enumerate(out_refs):
+            out_ref[:, :, loads] = turned[:, i].reshape(TAPS // STREAMS, hots, lanes)
 
 
 def tap_major(response):
     hots, loads, taps = response.shape
     block = 16
+    each = block // STREAMS
     return pl.pallas_call(
         functools.partial(tap_major_kernel, block),
         grid=(hots // block,),
-        in_specs=[pl.BlockSpec((block, loads, taps), lambda i: (i, 0, 0))],
-        out_specs=pl.BlockSpec((taps, block, loads), lambda i: (0, i, 0)),
-        out_shape=jax.ShapeDtypeStruct((taps, hots, loads), response.dtype),
+        in_specs=[
+            pl.BlockSpec((each, loads, taps), lambda i, part=part: (i * STREAMS + part, 0, 0))
+            for part in range(STREAMS)
+        ],
+        out_specs=[pl.BlockSpec((taps // STREAMS, block, loads), lambda i: (0, i, 0))] * STREAMS,
+        out_shape=[
+            jax.ShapeDtypeStruct((taps // STREAMS, hots, loads), response.dtype)
+        ] * STREAMS,
         scratch_shapes=[pltpu.VMEM((loads // 128, taps * block, 128), jnp.float32)],
         compiler_params=pltpu.CompilerParams(vmem_limit_bytes=40 * MIB),
         cost_estimate=pl.CostEstimate(
             flops=0, bytes_accessed=4 * response.size, transcendentals=0
         ),
         name="tap_major",
-    )(response)
+    )(*[response] * STREAMS)
 
 
 def tile_specs(hots, loads):
     return [
-        pl.BlockSpec((GROUP, hots, loads), lambda i, part=part: (i * STREAMS + part, 0, 0))
-        for part in range(STREAMS)
+        pl.BlockSpec((GROUP, hots, loads), lambda i: (i, 0, 0))
+        for _ in range(STREAMS)
     ]
 
 
@@ -80,21 +92,21 @@
 
 
 def strain_product(tiles, signal):
-    taps, hots, loads = tiles.shape
+    _, hots, loads = tiles[0].shape
     odd = jnp.concatenate([signal[CASES:], signal[:CASES]])
     whole = pl.BlockSpec((COLS, loads), lambda i: (0, 0))
     return pl.pallas_call(
         strain_kernel,
-        grid=(taps // STEP_TAPS,),
+        grid=(TAPS // STEP_TAPS,),
         in_specs=[whole, whole, *tile_specs(hots, loads)],
         out_specs=pl.BlockSpec((SEG_COLS, hots), lambda i: (0, 0)),
         out_shape=jax.ShapeDtypeStruct((SEG_COLS, hots), jnp.float32),
         compiler_params=pltpu.CompilerParams(vmem_limit_bytes=40 * MIB),
         cost_estimate=pl.CostEstimate(
-            flops=2 * SEG_COLS * tiles.size, bytes_accessed=2 * tiles.size, transcendentals=0
+            flops=2 * SEG_COLS * TAPS * hots * loads, bytes_accessed=2 * TAPS * hots * loads, transcendentals=0
         ),
         name="strain_product",
-    )(signal, odd, *[tiles] * STREAMS)
+    )(signal, odd, *tiles)
 
 
 def gradient_kernel(hots, strains_ref, *refs):
@@ -118,7 +130,7 @@
 
 
 def load_product(tiles, strains, parts):
-    taps, hots, loads = tiles.shape
+    _, hots, loads = tiles[0].shape
     rows = -(-COLS // (8 * parts)) * 8 * parts
     stacked = jnp.concatenate(
         [
@@ -132,7 +144,7 @@
     )
     return pl.pallas_call(
         functools.partial(gradient_kernel, hots),
-        grid=(taps // STEP_TAPS,),
+        grid=(TAPS // STEP_TAPS,),
         in_specs=[
             pl.BlockSpec((WINDOW, GROUP * hots), lambda i: (0, 0)),
             *tile_specs(hots, loads),
@@ -142,10 +154,10 @@
         scratch_shapes=[pltpu.VMEM((max(rows, COLS + 16), loads), jnp.float32)],
         compiler_params=pltpu.CompilerParams(vmem_limit_bytes=40 * MIB),
         cost_estimate=pl.CostEstimate(
-            flops=2 * WINDOW * tiles.size, bytes_accessed=2 * tiles.size, transcendentals=0
+            flops=2 * WINDOW * TAPS * hots * loads, bytes_accessed=2 * TAPS * hots * loads, transcendentals=0
         ),
         name="load_product",
-    )(stacked, *[tiles] * STREAMS)
+    )(stacked, *tiles)
 
 
 def greet(peers):
@@ -279,7 +291,7 @@
         ),
         name="image_sum",
     )(terms, jnp.broadcast_to(norm, tile))
-    return image, step[0, 0]
+    return image, step
 
 
 def hot_sum_kernel(count, in_ref, out_ref, pair, held, parts, pair_sems, part_sems, gather_sems, swap_sems):
@@ -350,6 +362,43 @@
     )(terms)
 
 
+def update_kernel(step_ref, forces_ref, gradient_ref, residual_ref, image_ref, forces_out, residual_out):
+    step_size = step_ref[:1, :1]
+    forces_out[...] = forces_ref[...].astype(jnp.float32) + step_size * gradient_ref[:COLS, :].T
+
+    @pl.when(pl.program_id(0) == 0)
+    def _():
+        residual_out[...] = (residual_ref[...] - step_size * image_ref[...]).T
+
+
+def update(step, forces, gradient, residual, image):
+    loads, hots = forces.shape[0], residual.shape[1]
+    block = 128
+
+    def whole(array):
+        return pl.BlockSpec(array.shape, lambda i: (0, 0))
+
+    by_load = pl.BlockSpec((block, COLS), lambda i: (i, 0))
+    return pl.pallas_call(
+        update_kernel,
+        grid=(loads // block,),
+        in_specs=[
+            whole(step),
+            by_load,
+            pl.BlockSpec((gradient.shape[0], block), lambda i: (0, i)),
+            whole(residual),
+            whole(image),
+        ],
+        out_specs=[by_load, pl.BlockSpec((hots, SEG_COLS), lambda i: (0, 0))],
+        out_shape=[
+            jax.ShapeDtypeStruct((loads, COLS), jnp.float32),
+            jax.ShapeDtypeStruct((hots, SEG_COLS), jnp.float32),
+        ],
+        compiler_params=pltpu.CompilerParams(vmem_limit_bytes=40 * MIB),
+        name="update",
+    )(step, forces, gradient, residual, image)
+
+
 def body(loads, hots, response, forces, measured):
     tiles = tap_major(response)
     strains = load_sum(strain_product(tiles, forces.T), loads)
@@ -358,9 +407,8 @@
     gradient = padded[:COLS]
     norm = jnp.sum(gradient * gradient)
     terms = strain_product(tiles, gradient.astype(jnp.bfloat16))
-    image, step_size = image_sum(terms, norm, loads, hots)
-    updated_forces = forces.astype(jnp.float32) + step_size * gradient.T
-    return updated_forces, (residual - step_size * image).T
+    image, step = image_sum(terms, norm, loads, hots)
+    return tuple(update(step, forces, padded, residual, image))
 
 
 def solution(mesh):

time: 199 us -> 193 us (0.970)
  other arithmetic: 7 us -> 1.64 us
  Pallas kernels: 181 us -> 178 us
  local copies, waits for them, and re-layouts: 9.01 us -> 11.7 us
    add x1 -> x0, other arithmetic: 3.97 us -> none  [body(): updated_forces = forces.astype(jnp.float32) + step_size * gradient.T]
    unnamed x12, local copies, waits for them, and re-layouts: 7.75 us -> 10.8 us
    pallas_call x1, Pallas kernels: 37.2 us -> 34.9 us  [tap_major(): pl.pallas_call(functools.partial(tap_major_kernel, block), grid=(hots //...]
    pallas_call x3 -> x4, Pallas kernels: 55.2 us -> 54.2 us  [the longest x2 33.3 us: strain_product(): pl.pallas_call(strain_kernel, grid=(TAPS // STEP_TAPS,), in_specs=[whole,...]
where the time goes in v3:
time: 193 us; the launch traced here: 192 us
  Pallas kernels  178 us (92%)
  local copies, waits for them, and re-layouts  11.7 us (6%)
    pallas_call x1, Pallas kernels, hot_sum(): pl.pallas_call(functools.partial(hot_sum_kernel, count), in_specs=[pl.Blo...  41.1 us
    pallas_call x1, Pallas kernels, tap_major(): pl.pallas_call(functools.partial(tap_major_kernel, block), grid=(hots //...  34.9 us
    pallas_call x2, Pallas kernels, strain_product(): pl.pallas_call(strain_kernel, grid=(TAPS // STEP_TAPS,), in_specs=[whole,...  33.3 us
    pallas_call x1, Pallas kernels, image_sum(): pl.pallas_call(functools.partial(image_sum_kernel, loads, hots), in_specs...  25.2 us
    pallas_call x1, Pallas kernels, load_sum(): pl.pallas_call(functools.partial(load_sum_kernel, count), in_specs=[pl.Bl...  22.3 us
    pallas_call x1, Pallas kernels, load_product(): pl.pallas_call(functools.partial(gradient_kernel, hots), grid=(TAPS // ST...  17.8 us
    unnamed x12, local copies, waits for them, and re-layouts  10.8 us

profile of v3, /device:TPU:0, one launch (start us, length us, event | category | flops | bytes accessed | tf_op | source)
XLA Modules:
  0.0 191.8 jit_solution(1323224192443210489)
XLA Ops:
  0.6 0.0 copy-start
  0.6 34.9 %tap_major.1 = (bf16[32,256,512]{2,1,0:T(8,128)(2,1)S(1)}, bf16[32,256,512]{2,1,0:T(8,128)(2,1)}, bf16[32,256,512]{2,1,0:T(8,128)(2,1)}, bf16[32,256,512]{2,1,0:T(8,128)(2,1)}) custom-call(bf16[256,512,128]{2,1,0:T(8,128)(2,1)} %refs_3_.1, bf16[256,512,128]{2,1,0:T(8,128)(2,1)} %refs_3_.1, bf16[256,512,128]{2,1,0:T(8,128)(2,1)} %refs_3_.1, ...), custom_call_target="tpu_custom_call" | custom-call | bytes 67108864 | tf_op jit(solution)/shard_map/tap_major/pallas_call | solution.py:44
  35.6 0.0 copy-start.1
  35.6 3.2 %copy-done.1 = bf16[32,256,512]{2,1,0:T(8,128)(2,1)} copy-done((bf16[32,256,512]{2,1,0:T(8,128)(2,1)}, bf16[32,256,512]{2,1,0:T(8,128)(2,1)S(1)}, u32[]{:S(2)}) %copy-start.1) | copy-done | bytes 8388632
  38.8 0.0 copy-done
  38.8 0.7 copy.6
  39.5 0.1 slice.16
  39.6 0.1 pad_maximum_fusion.odd_ref
  39.7 0.0 copy-start.2
  39.7 3.4 %copy-done.2 = bf16[32,256,512]{2,1,0:T(8,128)(2,1)S(1)} copy-done((bf16[32,256,512]{2,1,0:T(8,128)(2,1)S(1)}, bf16[32,256,512]{2,1,0:T(8,128)(2,1)}, u32[]{:S(2)}) %copy-start.2) | copy-done | bytes 8388632
  43.1 0.0 copy-start.4
  43.1 16.7 %strain_product.2.in_ref = f32[384,256]{1,0:T(8,128)S(1)} custom-call(bf16[1408,512]{1,0:T(8,128)(2,1)S(1)} %bitcast.6, bf16[1408,512]{1,0:T(8,128)(2,1)S(1)} %pad_maximum_fusion.odd_ref, bf16[32,256,512]{2,1,0:T(8,128)(2,1)S(1)} %copy-done.2, bf16[32,256,512]{2,1,0:T(8,128)(2,1)} %get-tuple-element.9.refs_1_, ...), custom_call_target="tpu_custom_call" | custom-call | flops 12884901888 | bytes 33554432 | tf_op jit(solution)/shard_map/strain_product/pallas_call | solution.py:98
  59.8 22.3 %load_sum.1 = f32[384,256]{1,0:T(8,128)S(1)} custom-call(f32[384,256]{1,0:T(8,128)S(1)} %strain_product.2.in_ref), custom_call_target="tpu_custom_call" | custom-call | tf_op jit(solution)/shard_map/load_sum/pallas_call | solution.py:229
  82.0 0.0 copy-done.4
  82.0 0.2 copy.5
  82.2 0.1 fusion.9
  82.3 0.1 fusion.7.strains_ref
  82.3 0.0 copy-start.3
  82.3 3.4 %copy-done.3 = bf16[32,256,512]{2,1,0:T(8,128)(2,1)S(1)} copy-done((bf16[32,256,512]{2,1,0:T(8,128)(2,1)S(1)}, bf16[32,256,512]{2,1,0:T(8,128)(2,1)}, u32[]{:S(2)}) %copy-start.3) | copy-done | bytes 8388632
  85.7 17.8 %load_product.1.in_ref = f32[1408,512]{1,0:T(8,128)S(1)} custom-call(bf16[416,1024]{1,0:T(8,128)(2,1)S(1)} %fusion.7.strains_ref, bf16[32,256,512]{2,1,0:T(8,128)(2,1)S(1)} %copy-done.3, bf16[32,256,512]{2,1,0:T(8,128)(2,1)} %get-tuple-element.9.refs_1_, bf16[32,256,512]{2,1,0:T(8,128)(2,1)} %get-tuple-element.10.refs_2_, ...), custom_call_target="tpu_custom_call" | custom-call | flops 13958643712 | bytes 33554432 | tf_op jit(solution)/shard_map/load_product/pallas_call | solution.py:145
  103.5 41.1 %hot_sum.1.gradient_ref = f32[1408,512]{1,0:T(8,128)S(1)} custom-call(f32[1408,512]{1,0:T(8,128)S(1)} %load_product.1.in_ref), custom_call_target="tpu_custom_call" | custom-call | tf_op jit(solution)/shard_map/hot_sum/pallas_call | solution.py:344
  144.6 1.3 multiply_reduce_fusion
  145.9 0.1 slice.18
  146.0 0.1 pad_maximum_fusion.1.odd_ref
  146.1 16.6 %strain_product.3.in_ref = f32[384,256]{1,0:T(8,128)S(1)} custom-call(bf16[1408,512]{1,0:T(8,128)(2,1)S(1)} %get-tuple-element.17.even_ref, bf16[1408,512]{1,0:T(8,128)(2,1)S(1)} %pad_maximum_fusion.1.odd_ref, bf16[32,256,512]{2,1,0:T(8,128)(2,1)S(1)} %copy-done.3, bf16[32,256,512]{2,1,0:T(8,128)(2,1)} %get-tuple-element.9.refs_1_, ...), custom_call_target="tpu_custom_call" | custom-call | flops 12884901888 | bytes 33554432 | tf_op jit(solution)/shard_map/strain_product/pallas_call | solution.py:98
  162.8 0.6 broadcast_in_dim.3.norm_ref
  163.4 25.2 %image_sum.1 = (f32[384,256]{1,0:T(8,128)S(1)}, f32[8,128]{1,0:T(8,128)S(1)}) custom-call(f32[384,256]{1,0:T(8,128)S(1)} %strain_product.3.in_ref, f32[8,128]{1,0:T(8,128)S(1)} %broadcast_in_dim.3.norm_ref), custom_call_target="tpu_custom_call" | custom-call | tf_op jit(solution)/shard_map/image_sum/pallas_call | solution.py:273
  188.6 3.2 %update.1 = (f32[512,1408]{1,0:T(8,128)}, f32[256,384]{1,0:T(8,128)}) custom-call(f32[8,128]{1,0:T(8,128)S(1)} %get-tuple-element.12.step_ref, bf16[512,1408]{1,0:T(8,128)(2,1)S(1)} %copy-done, f32[1408,512]{1,0:T(8,128)S(1)} %hot_sum.1.gradient_ref, f32[384,256]{1,0:T(8,128)S(1)} %get-tuple-element.15.residual_ref, f32[384,256]{1,0:T(8,128)S(1)} %get-tuple-element.13.image_ref), custom_call_target="tpu_custom_call" | custom-call | tf_op jit(solution)/shard_map/update/pallas_call | solution.py:382
  (2 shorter events, 0.0 us)
Async XLA Ops:
  0.6 38.2 %copy-start = (bf16[512,1408]{1,0:T(8,128)(2,1)S(1)}, bf16[512,1408]{1,0:T(8,128)(2,1)}, u32[]{:S(2)}) copy-start(bf16[512,1408]{1,0:T(8,128)(2,1)} %forces_ref.1) | copy-start | bytes 4325380
  35.6 3.2 %copy-start.1 = (bf16[32,256,512]{2,1,0:T(8,128)(2,1)}, bf16[32,256,512]{2,1,0:T(8,128)(2,1)S(1)}, u32[]{:S(2)}) copy-start(bf16[32,256,512]{2,1,0:T(8,128)(2,1)S(1)} %get-tuple-element.8.refs_0_) | copy-start | bytes 25165828
  39.7 3.4 %copy-start.2 = (bf16[32,256,512]{2,1,0:T(8,128)(2,1)S(1)}, bf16[32,256,512]{2,1,0:T(8,128)(2,1)}, u32[]{:S(2)}) copy-start(bf16[32,256,512]{2,1,0:T(8,128)(2,1)} %copy-done.1) | copy-start | bytes 25165828
  43.1 38.9 %copy-start.4 = (f32[256,384]{1,0:T(8,128)S(1)}, f32[256,384]{1,0:T(8,128)}, u32[]{:S(2)}) copy-start(f32[256,384]{1,0:T(8,128)} %param.5) | copy-start | bytes 1179652
  82.3 3.4 %copy-start.3 = (bf16[32,256,512]{2,1,0:T(8,128)(2,1)S(1)}, bf16[32,256,512]{2,1,0:T(8,128)(2,1)}, u32[]{:S(2)}) copy-start(bf16[32,256,512]{2,1,0:T(8,128)(2,1)} %copy-done.1) | copy-start | bytes 25165828

commit v4 on v3

--- a/solution.py
+++ b/solution.py
@@ -53,7 +53,7 @@
             jax.ShapeDtypeStruct((taps // STREAMS, hots, loads), response.dtype)
         ] * STREAMS,
         scratch_shapes=[pltpu.VMEM((loads // 128, taps * block, 128), jnp.float32)],
-        compiler_params=pltpu.CompilerParams(vmem_limit_bytes=40 * MIB),
+        compiler_params=pltpu.CompilerParams(vmem_limit_bytes=56 * MIB),
         cost_estimate=pl.CostEstimate(
             flops=0, bytes_accessed=4 * response.size, transcendentals=0
         ),
@@ -101,7 +101,7 @@
         in_specs=[whole, whole, *tile_specs(hots, loads)],
         out_specs=pl.BlockSpec((SEG_COLS, hots), lambda i: (0, 0)),
         out_shape=jax.ShapeDtypeStruct((SEG_COLS, hots), jnp.float32),
-        compiler_params=pltpu.CompilerParams(vmem_limit_bytes=40 * MIB),
+        compiler_params=pltpu.CompilerParams(vmem_limit_bytes=56 * MIB),
         cost_estimate=pl.CostEstimate(
             flops=2 * SEG_COLS * TAPS * hots * loads, bytes_accessed=2 * TAPS * hots * loads, transcendentals=0
         ),
@@ -152,7 +152,7 @@
         out_specs=pl.BlockSpec((rows, loads), lambda i: (0, 0)),
         out_shape=jax.ShapeDtypeStruct((rows, loads), jnp.float32),
         scratch_shapes=[pltpu.VMEM((max(rows, COLS + 16), loads), jnp.float32)],
-        compiler_params=pltpu.CompilerParams(vmem_limit_bytes=40 * MIB),
+        compiler_params=pltpu.CompilerParams(vmem_limit_bytes=56 * MIB),
         cost_estimate=pl.CostEstimate(
             flops=2 * WINDOW * TAPS * hots * loads, bytes_accessed=2 * TAPS * hots * loads, transcendentals=0
         ),
@@ -236,7 +236,7 @@
             pltpu.SemaphoreType.DMA((4, count - 1)),
         ],
         compiler_params=pltpu.CompilerParams(
-            collective_id=0, has_side_effects=True, vmem_limit_bytes=40 * MIB
+            collective_id=0, has_side_effects=True, vmem_limit_bytes=56 * MIB
         ),
         name="load_sum",
     )(terms)
@@ -287,7 +287,7 @@
             pltpu.SemaphoreType.DMA((2, hots - 1)),
         ],
         compiler_params=pltpu.CompilerParams(
-            collective_id=1, has_side_effects=True, vmem_limit_bytes=40 * MIB
+            collective_id=1, has_side_effects=True, vmem_limit_bytes=56 * MIB
         ),
         name="image_sum",
     )(terms, jnp.broadcast_to(norm, tile))
@@ -356,7 +356,7 @@
             pltpu.SemaphoreType.DMA((2, chips)),
         ],
         compiler_params=pltpu.CompilerParams(
-            collective_id=2, has_side_effects=True, vmem_limit_bytes=40 * MIB
+            collective_id=2, has_side_effects=True, vmem_limit_bytes=56 * MIB
         ),
         name="hot_sum",
     )(terms)
@@ -394,7 +394,7 @@
             jax.ShapeDtypeStruct((loads, COLS), jnp.float32),
             jax.ShapeDtypeStruct((hots, SEG_COLS), jnp.float32),
         ],
-        compiler_params=pltpu.CompilerParams(vmem_limit_bytes=40 * MIB),
+        compiler_params=pltpu.CompilerParams(vmem_limit_bytes=56 * MIB),
         name="update",
     )(step, forces, gradient, residual, image)
 

time: 193 us -> 212 us (1.098)
  Pallas kernels: 178 us -> 198 us
  local copies, waits for them, and re-layouts: 11.7 us -> 2.47 us
  other arithmetic: 1.64 us -> 9.55 us
    unnamed x12 -> x10, local copies, waits for them, and re-layouts: 10.8 us -> 1.05 us
    pallas_call x2, Pallas kernels: 33.3 us -> 40.6 us  [strain_product(): pl.pallas_call(strain_kernel, grid=(TAPS // STEP_TAPS,), in_specs=[whole,...]
    pallas_call x1, Pallas kernels: 41.1 us -> 44.4 us  [hot_sum(): pl.pallas_call(functools.partial(hot_sum_kernel, count), in_specs=[pl.Blo...]
    pallas_call x1, Pallas kernels: 17.8 us -> 21 us  [load_product(): pl.pallas_call(functools.partial(gradient_kernel, hots), grid=(TAPS // ST...]
    reduce_sum x1, other arithmetic: 1.34 us -> 4.06 us  [body(): norm = jnp.sum(gradient * gradient)]
    concatenate x2, other arithmetic: 0.19 us -> 2.74 us  [strain_product(): odd = jnp.concatenate([signal[CASES:], signal[:CASES]])]
    pallas_call x1, Pallas kernels: 3.17 us -> 5.34 us  [update(): pl.pallas_call(update_kernel, grid=(loads // block,), in_specs=[whole(ste...]
where the time goes in v4:
time: 212 us; the launch traced here: 211 us
  Pallas kernels  198 us (93%)
  other arithmetic  9.55 us (5%)
  local copies, waits for them, and re-layouts  2.47 us (1%)
    pallas_call x1, Pallas kernels, hot_sum(): pl.pallas_call(functools.partial(hot_sum_kernel, count), in_specs=[pl.Blo...  44.4 us
    pallas_call x2, Pallas kernels, strain_product(): pl.pallas_call(strain_kernel, grid=(TAPS // STEP_TAPS,), in_specs=[whole,...  40.6 us
    pallas_call x1, Pallas kernels, tap_major(): pl.pallas_call(functools.partial(tap_major_kernel, block), grid=(hots //...  36.3 us
    pallas_call x1, Pallas kernels, image_sum(): pl.pallas_call(functools.partial(image_sum_kernel, loads, hots), in_specs...  26.8 us
    pallas_call x1, Pallas kernels, load_sum(): pl.pallas_call(functools.partial(load_sum_kernel, count), in_specs=[pl.Bl...  24 us
    pallas_call x1, Pallas kernels, load_product(): pl.pallas_call(functools.partial(gradient_kernel, hots), grid=(TAPS // ST...  21 us
    pallas_call x1, Pallas kernels, update(): pl.pallas_call(update_kernel, grid=(loads // block,), in_specs=[whole(ste...  5.34 us

profile of v4, /device:TPU:0, one launch (start us, length us, event | category | flops | bytes accessed | tf_op | source)
XLA Modules:
  0.0 211.2 jit_solution(16911874120850990126)
XLA Ops:
  0.6 0.0 copy-start.2
  0.6 36.3 %tap_major.1 = (bf16[32,256,512]{2,1,0:T(8,128)(2,1)}, bf16[32,256,512]{2,1,0:T(8,128)(2,1)}, bf16[32,256,512]{2,1,0:T(8,128)(2,1)}, bf16[32,256,512]{2,1,0:T(8,128)(2,1)}) custom-call(bf16[256,512,128]{2,1,0:T(8,128)(2,1)} %refs_3_.1, bf16[256,512,128]{2,1,0:T(8,128)(2,1)} %refs_3_.1, bf16[256,512,128]{2,1,0:T(8,128)(2,1)} %refs_3_.1, ...), custom_call_target="tpu_custom_call" | custom-call | bytes 67108864 | tf_op jit(solution)/shard_map/tap_major/pallas_call | solution.py:44
  37.0 0.0 copy-done.2
  37.0 0.7 copy.6
  37.7 0.0 copy-start.1
  37.7 0.1 slice.16
  37.8 1.4 pad_maximum_fusion.odd_ref
  39.2 0.1 copy-done.1
  39.3 0.0 copy-start.3
  39.3 20.3 %strain_product.2.in_ref = f32[384,256]{1,0:T(8,128)} custom-call(bf16[1408,512]{1,0:T(8,128)(2,1)} %bitcast.6, bf16[1408,512]{1,0:T(8,128)(2,1)} %pad_maximum_fusion.odd_ref, bf16[32,256,512]{2,1,0:T(8,128)(2,1)} %get-tuple-element.8.refs_0_, bf16[32,256,512]{2,1,0:T(8,128)(2,1)} %get-tuple-element.9.refs_1_, ...), custom_call_target="tpu_custom_call" | custom-call | flops 12884901888 | bytes 33554432 | tf_op jit(solution)/shard_map/strain_product/pallas_call | solution.py:98
  59.6 24.0 %load_sum.1 = f32[384,256]{1,0:T(8,128)} custom-call(f32[384,256]{1,0:T(8,128)} %strain_product.2.in_ref), custom_call_target="tpu_custom_call" | custom-call | tf_op jit(solution)/shard_map/load_sum/pallas_call | solution.py:229
  83.6 0.0 copy-done.3
  83.6 0.2 copy.5
  83.8 1.8 fusion.9
  85.6 0.9 fusion.7.strains_ref
  86.5 21.0 %load_product.1.in_ref = f32[1408,512]{1,0:T(8,128)} custom-call(bf16[416,1024]{1,0:T(8,128)(2,1)} %fusion.7.strains_ref, bf16[32,256,512]{2,1,0:T(8,128)(2,1)} %get-tuple-element.8.refs_0_, bf16[32,256,512]{2,1,0:T(8,128)(2,1)} %get-tuple-element.9.refs_1_, bf16[32,256,512]{2,1,0:T(8,128)(2,1)} %get-tuple-element.10.refs_2_, ...), custom_call_target="tpu_custom_call" | custom-call | flops 13958643712 | bytes 33554432 | tf_op jit(solution)/shard_map/load_product/pallas_call | solution.py:145
  107.5 44.4 %hot_sum.1.gradient_ref = f32[1408,512]{1,0:T(8,128)} custom-call(f32[1408,512]{1,0:T(8,128)} %load_product.1.in_ref), custom_call_target="tpu_custom_call" | custom-call | tf_op jit(solution)/shard_map/hot_sum/pallas_call | solution.py:344
  151.9 4.1 %multiply_reduce_fusion = (f32[]{:T(128)}, bf16[1408,512]{1,0:T(8,128)(2,1)S(1)}) fusion(f32[1408,512]{1,0:T(8,128)} %hot_sum.1.gradient_ref), kind=kLoop, calls=%fused_computation | loop fusion | flops 2162687 | bytes 4325380 | tf_op jit(solution)/shard_map/reduce_sum | solution.py:408
  156.0 0.0 copy-start
  156.0 0.1 slice.18
  156.1 1.4 pad_maximum_fusion.1.odd_ref
  157.5 0.1 copy-done
  157.5 20.3 %strain_product.3.in_ref = f32[384,256]{1,0:T(8,128)} custom-call(bf16[1408,512]{1,0:T(8,128)(2,1)} %copy-done, bf16[1408,512]{1,0:T(8,128)(2,1)} %pad_maximum_fusion.1.odd_ref, bf16[32,256,512]{2,1,0:T(8,128)(2,1)} %get-tuple-element.8.refs_0_, bf16[32,256,512]{2,1,0:T(8,128)(2,1)} %get-tuple-element.9.refs_1_, ...), custom_call_target="tpu_custom_call" | custom-call | flops 12884901888 | bytes 33554432 | tf_op jit(solution)/shard_map/strain_product/pallas_call | solution.py:98
  177.8 1.2 broadcast_in_dim.3.norm_ref
  179.0 26.8 %image_sum.1 = (f32[384,256]{1,0:T(8,128)}, f32[8,128]{1,0:T(8,128)}) custom-call(f32[384,256]{1,0:T(8,128)} %strain_product.3.in_ref, f32[8,128]{1,0:T(8,128)} %broadcast_in_dim.3.norm_ref), custom_call_target="tpu_custom_call" | custom-call | tf_op jit(solution)/shard_map/image_sum/pallas_call | solution.py:273
  205.8 5.3 %update.1 = (f32[512,1408]{1,0:T(8,128)}, f32[256,384]{1,0:T(8,128)}) custom-call(f32[8,128]{1,0:T(8,128)} %get-tuple-element.12.step_ref, bf16[512,1408]{1,0:T(8,128)(2,1)} %forces_ref.1, f32[1408,512]{1,0:T(8,128)} %hot_sum.1.gradient_ref, f32[384,256]{1,0:T(8,128)} %get-tuple-element.15.residual_ref, f32[384,256]{1,0:T(8,128)} %get-tuple-element.13.image_ref), custom_call_target="tpu_custom_call" | custom-call | tf_op jit(solution)/shard_map/update/pallas_call | solution.py:382
  (2 shorter events, 0.0 us)
Async XLA Ops:
  0.6 36.4 %copy-start.2 = (bf16[512,1408]{1,0:T(8,128)(2,1)S(1)}, bf16[512,1408]{1,0:T(8,128)(2,1)}, u32[]{:S(2)}) copy-start(bf16[512,1408]{1,0:T(8,128)(2,1)} %forces_ref.1) | copy-start | bytes 4325380
  37.7 1.6 copy-start.1
  39.3 44.3 %copy-start.3 = (f32[256,384]{1,0:T(8,128)S(1)}, f32[256,384]{1,0:T(8,128)}, u32[]{:S(2)}) copy-start(f32[256,384]{1,0:T(8,128)} %param.5) | copy-start | bytes 1179652
  156.0 1.6 copy-start
